TPU v7x, 32 devices: a whole 2x2x4 slice. The times are simulated.
32 devices in a mesh: dp: 4 (over z), context: 8 (over y, x, core).
Axes of the slice: x: 2, y: 2, z: 4, core: 2. Of those that a mesh axis runs over, the one named last changes fastest.
Arguments:
- query_in: bfloat16 [4, 4096, 1024], P('dp', 'context'), may hold values from -6 to 6
- key_in: bfloat16 [4, 4096, 1024], P('dp', 'context'), may hold values from -6 to 6
- value_in: bfloat16 [4, 4096, 1024], P('dp', 'context'), may hold values from -6 to 6
- out_grad: bfloat16 [4, 4096, 2048], P('dp', 'context'), may hold values from -6 to 6
- out_weight: bfloat16 [1024, 2048], P('context'), may hold values from -0.1875 to 0.1875
Outputs:
- output: bfloat16 [4, 4096, 2048], P('dp', 'context')
- query_grad: bfloat16 [4, 4096, 1024], P('dp', 'context')
- key_grad: bfloat16 [4, 4096, 1024], P('dp', 'context')
- value_grad: bfloat16 [4, 4096, 1024], P('dp', 'context')
- weight_grad: float32 [1024, 2048], P('context')
All inputs are finite; a program needn't handle non-finite values.
Results may differ from a plain program's by a relative error of at most 0.025.
Values may be sent and summed in bfloat16 or wider, within the bound.
A program may use at most 192 MiB of HBM per device.

v0:
```python
import math

import jax
import jax.numpy as jnp
from jax import lax
from jax.sharding import PartitionSpec as P

HEADS = 8
HEAD_DIM = 128


def prefix(value, axis, join, neutral, backward):
    count, mine = (lax.axis_size(axis), lax.axis_index(axis))
    pieces = lax.all_gather(value, axis)
    if backward:
        pieces = pieces[::-1]
        mine = count - 1 - mine
    so_far = jnp.full_like(value, 0) + jnp.asarray(neutral, value.dtype)

    def turn(position, so_far):
        longer = join(so_far, pieces[position])
        return jnp.where(position < mine, longer, so_far)

    return lax.fori_loop(0, count - 1, turn, so_far)


def add_state(earlier, later):
    return earlier + later


def on_device(query_in, key_in, value_in, out_grad, out_weight):
    tok_rows = query_in.shape[1]
    head_width = query_in.shape[2]
    contexts = lax.axis_size("context")
    groups = lax.axis_size("dp")
    att_scale = 1.0 / math.sqrt(HEAD_DIM * tok_rows * contexts)
    grad_scale = 1.0 / math.sqrt(tok_rows * contexts * groups)
    split_heads = (tok_rows, HEADS, HEAD_DIM)
    queries = query_in[0].reshape(split_heads)
    keys_here = key_in[0].reshape(split_heads)
    values_here = value_in[0].reshape(split_heads)
    grad_flat = out_grad[0]
    full_weight = lax.all_gather(out_weight, "context", axis=0, tiled=True)
    head_grad = lax.dot_general(
        grad_flat, full_weight, (((1,), (1,)), ((), ())), preferred_element_type=jnp.float32
    ).astype(jnp.bfloat16)
    grad_heads = head_grad.reshape(split_heads)
    kv_block = jnp.einsum(
        "shd,she->hde", keys_here, values_here, preferred_element_type=jnp.float32
    )
    qg_block = jnp.einsum("thd,the->hde", queries, grad_heads, preferred_element_type=jnp.float32)
    blank_state = jnp.zeros_like(kv_block)
    kv_prior = prefix(kv_block, "context", add_state, blank_state, False)
    qg_later = prefix(qg_block, "context", add_state, blank_state, True)
    kv_before = kv_prior.astype(jnp.bfloat16)
    qg_after = qg_later.astype(jnp.bfloat16)
    positions = lax.broadcasted_iota(jnp.int32, (tok_rows, tok_rows), 0)
    sources = lax.broadcasted_iota(jnp.int32, (tok_rows, tok_rows), 1)
    causal = (positions >= sources)[None]
    scores = (
        jnp.einsum("thd,shd->hts", queries, keys_here, preferred_element_type=jnp.float32)
        * att_scale
    )
    scores = jnp.where(causal, scores, 0.0).astype(jnp.bfloat16)
    attended = jnp.einsum(
        "hts,shd->thd", scores, values_here, preferred_element_type=jnp.float32
    ) + att_scale * jnp.einsum(
        "thd,hde->the", queries, kv_before, preferred_element_type=jnp.float32
    )
    attended = attended.astype(jnp.bfloat16).reshape(tok_rows, head_width)
    output = jnp.dot(attended, full_weight, preferred_element_type=jnp.float32).astype(jnp.bfloat16)
    back_scores = (
        jnp.einsum("the,she->hts", grad_heads, values_here, preferred_element_type=jnp.float32)
        * att_scale
    )
    back_scores = jnp.where(causal, back_scores, 0.0).astype(jnp.bfloat16)
    query_grad = jnp.einsum(
        "hts,shd->thd", back_scores, keys_here, preferred_element_type=jnp.float32
    ) + att_scale * jnp.einsum(
        "the,hde->thd", grad_heads, kv_before, preferred_element_type=jnp.float32
    )
    key_grad = jnp.einsum(
        "hts,thd->shd", back_scores, queries, preferred_element_type=jnp.float32
    ) + att_scale * jnp.einsum(
        "she,hde->shd", values_here, qg_after, preferred_element_type=jnp.float32
    )
    value_grad = jnp.einsum(
        "hts,the->she", scores, grad_heads, preferred_element_type=jnp.float32
    ) + att_scale * jnp.einsum(
        "shd,hde->she", keys_here, qg_after, preferred_element_type=jnp.float32
    )
    query_grad = query_grad.astype(jnp.bfloat16).reshape(tok_rows, head_width)
    key_grad = key_grad.astype(jnp.bfloat16).reshape(tok_rows, head_width)
    value_grad = value_grad.astype(jnp.bfloat16).reshape(tok_rows, head_width)
    group_part = lax.psum_scatter(
        (
            lax.dot_general(
                attended, grad_flat, (((0,), (0,)), ((), ())), preferred_element_type=jnp.float32
            )
            * grad_scale
        ).astype(jnp.bfloat16),
        "context",
        scatter_dimension=0,
        tiled=True,
    )
    weight_grad = lax.psum(group_part, "dp").astype(jnp.float32)
    return (output[None], query_grad[None], key_grad[None], value_grad[None], weight_grad)


def solution(mesh):
    placed = (
        P("dp", "context", None),
        P("dp", "context", None),
        P("dp", "context", None),
        P("dp", "context", None),
        P("context", None),
    )
    return jax.shard_map(
        on_device,
        mesh=mesh,
        in_specs=placed,
        out_specs=(
            P("dp", "context", None),
            P("dp", "context", None),
            P("dp", "context", None),
            P("dp", "context", None),
            P("context", None),
        ),
        check_vma=False,
    )
```

profile of v0, /device:TPU:0, one launch (start us, length us, event | category | flops | bytes accessed | tf_op | source)
XLA Modules:
  0.0 280.0 jit_solution(6247599951936864416)
XLA Ops:
  7.2 2.6 copy.59
  9.8 2.5 copy.58
  12.3 2.4 copy.35
  14.7 2.8 fusion.16
  17.6 2.5 copy.57
  20.1 5.0 %select_convert_fusion.1 = bf16[8,512,512]{2,1,0:T(8,128)(2,1)} fusion(pred[512,512]{1,0:T(8,128)(4,1)S(1)} %iota_compare_fusion, bf16[512,8,128]{2,1,0:T(8,128)(2,1)} %bitcast.82, bf16[512,8,128]{2,1,0:T(8,128)(2,1)} %bitcast.77), kind=kOutput, calls=%fused_computation.4 | convolution fusion | flops 543162368 | bytes 6553600 | tf_op jit(solution)/shard_map/thd,shd->hts/dot_general | solution.py:61
  25.2 31.9 %all-gather.8.cloned.1.call-done = f32[64,128,128]{2,1,0:T(8,128)} async-done(((f32[8,128,128]{2,1,0:T(8,128)}), f32[64,128,128]{2,1,0:T(8,128)}) %all-gather.8.cloned.1.call-update) | async-done | bytes 4194320 | tf_op jit(solution)/shard_map/all_gather | solution.py:14
  57.1 8.7 %while.28 = (s32[]{:T(128)}, f32[8,128,128]{2,1,0:T(8,128)S(1)}, s32[]{:T(128)}, f32[8,8,128,128]{3,2,1,0:T(8,128)}, s32[]{:T(128)}, /*index=5*/s32[]{:T(128)}) while((s32[]{:T(128)}, f32[8,128,128]{2,1,0:T(8,128)S(1)}, s32[]{:T(128)}, f32[8,8,128,128]{3,2,1,0:T(8,128)}, s32[]{:T(128)}, /*index=5*/s32[]{:T(128)}) %tuple.81), condition=%wide.region_1.2_spmd.clone, body=%wide.region_0.1_spmd.clone.sunk | while | flops 393220 | bytes 1572957 | solution.py:24
  57.1 1.2 add_select_fusion.4
  58.3 1.2 add_select_fusion.4
  59.6 1.2 add_select_fusion.4
  60.8 1.2 add_select_fusion.4
  62.1 1.2 add_select_fusion.4
  63.4 1.2 add_select_fusion.4
  64.6 1.2 add_select_fusion.4
  65.9 1.8 fusion.21
  67.7 3.7 %fusion.6 = bf16[512,8,128]{0,2,1:T(8,128)(2,1)S(1)} fusion(f32[8,128,512]{2,1,0:T(8,128)S(1)} %fusion.21, bf16[8,512,512]{2,1,0:T(8,128)(2,1)} %select_convert_fusion.1, bf16[512,8,128]{2,1,0:T(8,128)(2,1)S(1)} %bitcast.76), kind=kOutput, calls=%fused_computation.15 | convolution fusion | flops 538443776 | bytes 8388608 | tf_op jit(solution)/shard_map/hts,shd->thd/dot_general | solution.py:65
  71.4 1.0 copy-done.5
  72.4 4.3 %multiply_convert_fusion = bf16[1024,2048]{1,0:T(8,128)(2,1)} fusion(bf16[512,1024]{0,1:T(8,128)(2,1)S(1)} %bitcast.92, bf16[1,512,2048]{2,1,0:T(8,128)(2,1)S(1)} %copy-done), kind=kOutput, calls=%fused_computation.2 | convolution fusion | flops 2151677952 | bytes 7340032 | tf_op jit(solution)/shard_map/dot_general | solution.py:97
  77.5 50.7 %reduce-scatter.2.cloned.1.call-done = bf16[128,2048]{1,0:T(8,128)(2,1)} async-done(((bf16[1024,2048]{1,0:T(8,128)(2,1)}), bf16[128,2048]{1,0:T(8,128)(2,1)}) %reduce-scatter.2.cloned.1.call-update) | async-done | bytes 524304 | tf_op jit(solution)/shard_map/reduce_scatter | solution.py:95
  128.4 38.5 %all-gather.6.cloned.1.call-done = bf16[1024,2048]{1,0:T(8,128)(2,1)} async-done(((bf16[128,2048]{1,0:T(8,128)(2,1)}), bf16[1024,2048]{1,0:T(8,128)(2,1)}) %all-gather.6.cloned.1.call-update) | async-done | bytes 4194320 | tf_op jit(solution)/shard_map/all_gather | solution.py:43
  167.0 5.5 %fusion.7 = bf16[512,1024]{1,0:T(8,128)(2,1)} fusion(bf16[1024,2048]{1,0:T(8,128)(2,1)} %all-gather.6.cloned.1.call-done, bf16[1,512,2048]{2,1,0:T(8,128)(2,1)S(1)} %copy-done), kind=kOutput, calls=%fused_computation.17 | convolution fusion | flops 2148007936 | bytes 7340032 | tf_op jit(solution)/shard_map/dot_general | solution.py:44
  172.5 2.3 copy.56
  174.8 2.0 convolution_bitcast_fusion
  176.8 1.0 copy.46
  177.8 1.6 fusion.25
  179.5 3.2 %select_convert_fusion = bf16[8,512,512]{2,1,0:T(8,128)(2,1)S(1)} fusion(pred[512,512]{1,0:T(8,128)(4,1)S(1)} %iota_compare_fusion, bf16[512,8,128]{0,2,1:T(8,128)(2,1)} %bitcast.71, bf16[512,8,128]{2,1,0:T(8,128)(2,1)} %bitcast.74), kind=kOutput, calls=%fused_computation.3 | convolution fusion | flops 543162368 | bytes 6553600 | tf_op jit(solution)/shard_map/the,she->hts/dot_general | solution.py:73
  182.8 2.5 fusion.2
  185.2 2.3 copy.51
  187.5 4.7 %fusion.28 = f32[8,128,512]{2,1,0:T(8,128)} fusion(bf16[512,8,128]{0,2,1:T(8,128)(2,1)} %bitcast.72, bf16[8,512,512]{2,1,0:T(8,128)(2,1)} %select_convert_fusion.1), kind=kOutput, calls=%fused_computation.38 | convolution fusion | flops 536870912 | bytes 7340032 | tf_op jit(solution)/shard_map/hts,the->she/dot_general | solution.py:87
  192.2 3.8 %fusion = bf16[1,512,2048]{2,1,0:T(8,128)(2,1)} fusion(bf16[512,1024]{0,1:T(8,128)(2,1)S(1)} %bitcast.93, bf16[1024,2048]{1,0:T(8,128)(2,1)S(1)} %copy-done.7), kind=kOutput, calls=%fused_computation.6 | convolution fusion | flops 2148532224 | bytes 7340032 | tf_op jit(solution)/shard_map/dot_general | solution.py:71
  196.0 11.6 %all-reduce.2.cloned.1.call-done = bf16[128,2048]{1,0:T(8,128)(2,1)} async-done(((bf16[128,2048]{1,0:T(8,128)(2,1)}), bf16[128,2048]{1,0:T(8,128)(2,1)}) %all-reduce.2.cloned.1.call-update) | async-done | bytes 524304 | tf_op jit(solution)/shard_map/psum | solution.py:106
  207.6 2.1 convert_element_type.51
  209.7 36.5 %all-gather.10.cloned.1.call-done = f32[64,128,128]{2,1,0:T(8,128)} async-done(((f32[8,128,128]{2,1,0:T(8,128)}), f32[64,128,128]{2,1,0:T(8,128)}) %all-gather.10.cloned.1.call-update) | async-done | bytes 4194320 | tf_op jit(solution)/shard_map/all_gather | solution.py:14
  246.3 4.7 %rev.3 = f32[8,8,128,128]{3,2,1,0:T(8,128)} reverse(f32[8,8,128,128]{3,2,1,0:T(8,128)} %bitcast.84), dimensions={0} | reverse | bytes 8388608 | tf_op jit(solution)/shard_map/rev | solution.py:16
  250.9 8.7 %while.29 = (s32[]{:T(128)}, f32[8,128,128]{2,1,0:T(8,128)S(1)}, s32[]{:T(128)}, f32[8,8,128,128]{3,2,1,0:T(8,128)}, s32[]{:T(128)}, /*index=5*/s32[]{:T(128)}) while((s32[]{:T(128)}, f32[8,128,128]{2,1,0:T(8,128)S(1)}, s32[]{:T(128)}, f32[8,8,128,128]{3,2,1,0:T(8,128)}, s32[]{:T(128)}, /*index=5*/s32[]{:T(128)}) %tuple.68), condition=%wide.region_3.4_spmd.clone, body=%wide.region_2.3_spmd.clone.sunk | while | flops 393220 | bytes 1572957 | solution.py:24
  250.9 1.2 add_select_fusion.5
  252.2 1.2 add_select_fusion.5
  253.4 1.2 add_select_fusion.5
  254.7 1.2 add_select_fusion.5
  255.9 1.2 add_select_fusion.5
  257.2 1.2 add_select_fusion.5
  258.4 1.2 add_select_fusion.5
  259.7 1.8 fusion.13
  261.5 4.1 %fusion.1 = bf16[512,8,128]{0,2,1:T(8,128)(2,1)} fusion(f32[8,128,512]{2,1,0:T(8,128)S(1)} %fusion.13, bf16[8,512,512]{2,1,0:T(8,128)(2,1)} %copy-done.1, bf16[512,8,128]{2,1,0:T(8,128)(2,1)S(1)} %bitcast.80), kind=kOutput, calls=%fused_computation.8 | convolution fusion | flops 538443776 | bytes 8388608 | tf_op jit(solution)/shard_map/hts,thd->shd/dot_general | solution.py:82
  265.5 2.3 copy.52
  267.8 3.4 %add_convert_fusion = bf16[8,128,512]{2,1,0:T(8,128)(2,1)} fusion(f32[8,128,512]{2,1,0:T(8,128)} %fusion.28, bf16[512,8,128]{2,1,0:T(8,128)(2,1)} %bitcast.83, f32[8,128,128]{2,1,0:T(8,128)S(1)} %get-tuple-element.164), kind=kOutput, calls=%fused_computation.16 | convolution fusion | flops 135921664 | bytes 4718592 | tf_op jit(solution)/shard_map/shd,hde->she/dot_general | solution.py:89
  271.3 2.3 copy.53
  (28 shorter events, 1.3 us)
Async XLA Ops:
  7.2 65.2 %copy-start = (bf16[1,512,2048]{2,1,0:T(8,128)(2,1)S(1)}, bf16[1,512,2048]{2,1,0:T(8,128)(2,1)}, u32[]{:S(2)}) copy-start(bf16[1,512,2048]{2,1,0:T(8,128)(2,1)} %param.12) | copy-start | bytes 6291460
  7.2 49.9 %all-gather.8.cloned.1.call-start = ((), (), s32[]{:S(2)}) async-start(), calls=%async_computation.4 | async-start | bytes 4718592 | tf_op jit(solution)/shard_map/all_gather | solution.py:14
  17.5 110.7 %reduce-scatter.2.cloned.1.call-start = ((), (), s32[]{:S(2)}) async-start(), calls=%async_computation.2 | async-start | bytes 4718592 | tf_op jit(solution)/shard_map/reduce_scatter | solution.py:95
  65.8 1.8 copy-start.2
  71.4 1.0 copy-start.5
  76.7 90.3 %all-gather.6.cloned.1.call-start = ((), (), s32[]{:S(2)}) async-start(), calls=%async_computation.1 | async-start | bytes 4718592 | tf_op jit(solution)/shard_map/all_gather | solution.py:43
  77.4 130.2 %all-reduce.2.cloned.1.call-start = ((), (), s32[]{:S(2)}) async-start(), calls=%async_computation.3 | async-start | bytes 1048576 | tf_op jit(solution)/shard_map/psum | solution.py:106
  128.2 118.0 %all-gather.10.cloned.1.call-start = ((), (), s32[]{:S(2)}) async-start(), calls=%async_computation.5 | async-start | bytes 4718592 | tf_op jit(solution)/shard_map/all_gather | solution.py:14
  179.5 3.3 %copy-start.4 = (bf16[512,8,128]{0,2,1:T(8,128)(2,1)S(1)}, bf16[512,8,128]{0,2,1:T(8,128)(2,1)}, u32[]{:S(2)}) copy-start(bf16[512,8,128]{0,2,1:T(8,128)(2,1)} %copy.35) | copy-start | bytes 3145732
  182.8 2.5 copy-start.1
  187.5 4.7 %copy-start.6 = (bf16[512,8,128]{0,2,1:T(8,128)(2,1)S(1)}, bf16[512,8,128]{0,2,1:T(8,128)(2,1)}, u32[]{:S(2)}) copy-start(bf16[512,8,128]{0,2,1:T(8,128)(2,1)} %copy-done.5) | copy-start | bytes 3145732
  187.5 4.7 %copy-start.7 = (bf16[1024,2048]{1,0:T(8,128)(2,1)S(1)}, bf16[1024,2048]{1,0:T(8,128)(2,1)}, u32[]{:S(2)}) copy-start(bf16[1024,2048]{1,0:T(8,128)(2,1)} %all-gather.6.cloned.1.call-done) | copy-start | bytes 12582916
  259.7 1.8 copy-start.3
Sparse Core Ops, SparseCore 0:
  17.6 39.4 all-gather.7
  76.8 51.3 reduce-scatter.1
  130.2 36.6 all-gather.5
  169.3 38.2 all-reduce.1
  209.5 36.6 all-gather.9
where the time goes:
time: 281 us; the launch traced here: 280 us
  waiting for transfers between devices  170 us (60%)
  matrix products  50.2 us (18%)
  local copies, waits for them, and re-layouts  25.7 us (9%)
  other arithmetic  19.4 us (7%)
  between operations  13.9 us (5%)
    all_gather x2, waiting for transfers between devices, prefix(): pieces = lax.all_gather(value, axis)  68.5 us
    reduce_scatter x1, waiting for transfers between devices, on_device(): lax.psum_scatter((lax.dot_general(attended, grad_flat, (((0,), (0,)), (()...  50.7 us
    all_gather x1, waiting for transfers between devices, on_device(): full_weight = lax.all_gather(out_weight, 'context', axis=0, tiled=True)  38.5 us
    select_n x14, other arithmetic, turn(): return jnp.where(position < mine, longer, so_far)  17.2 us
    unnamed x22, local copies, waits for them, and re-layouts  15.4 us
    psum x1, waiting for transfers between devices, on_device(): weight_grad = lax.psum(group_part, 'dp').astype(jnp.float32)  11.6 us
  transfers between devices with their start and end apart: 5, of which 5 were waited for; matrix products, arithmetic and copies ran while one was open for 14% of the time, Pallas kernels for 0%

commit v1 on v0

v1 whole, which is shorter than its diff:
```python
import functools
import math

import jax
import jax.numpy as jnp
from jax import lax
from jax.experimental import pallas as pl
from jax.experimental.pallas import tpu as pltpu
from jax.sharding import PartitionSpec as P

HEADS = 8
HEAD_DIM = 128
F32 = jnp.float32
BF16 = jnp.bfloat16


def dot_nn(a, b):
    return lax.dot_general(a, b, (((1,), (0,)), ((), ())), preferred_element_type=F32)


def dot_nt(a, b):
    return lax.dot_general(a, b, (((1,), (1,)), ((), ())), preferred_element_type=F32)


def dot_tn(a, b):
    return lax.dot_general(a, b, (((0,), (0,)), ((), ())), preferred_element_type=F32)


def loop(count, body):
    lax.fori_loop(0, count, lambda i, _: (body(i), 0)[1], 0)


def kernel(
    n, g, q_ref, k_ref, v_ref, og_ref, w_ref, out_ref, qgrad_ref, kgrad_ref, vgrad_ref, wgrad_ref,
    wfull, kv_send, kv_recv, kv_pref, kvb, qg_send, qg_recv, qg_pref, qga,
    scores, intra, att, att_t, hg, wchunk, keep, sib_send, sib_recv, x_send, x_recv,
    z_send, z_recv, z2_send, z2_recv,
    s_kv1, r_kv1, s_kv2, r_kv2, s_qg1, r_qg1, s_qg2, r_qg2,
    s_w, s_wf, r_w, s_sib, r_sib, s_x, r_x, s_z, r_z, s_z2, r_z2,
):
    me, z = lax.axis_index("context"), lax.axis_index("dp")
    nc = n // 2
    chip, core = me // 2, lax.rem(me, 2)
    sibling = chip * 2 + 1 - core
    tok, width = q_ref.shape
    model = og_ref.shape[1]
    rows = width // n
    cols = model // g
    att_scale = 1.0 / math.sqrt(HEAD_DIM * tok * n)
    grad_scale = 1.0 / math.sqrt(tok * n * g)

    def head(h):
        return pl.ds(pl.multiple_of(h * HEAD_DIM, HEAD_DIM), HEAD_DIM)

    def part(d):
        return pl.ds(pl.multiple_of(d * rows, rows), rows)

    def column(q):
        return pl.ds(pl.multiple_of(q * cols, cols), cols)

    def to(src, dst, ssem, rsem, device):
        return pltpu.make_async_remote_copy(
            src_ref=src, dst_ref=dst, send_sem=ssem, recv_sem=rsem,
            device_id=(z, device), device_id_type=pl.DeviceIdType.MESH,
        )

    def to_z(src, dst, ssem, rsem, group):
        return pltpu.make_async_remote_copy(
            src_ref=src, dst_ref=dst, send_sem=ssem, recv_sem=rsem,
            device_id=(group, me), device_id_type=pl.DeviceIdType.MESH,
        )

    barrier = pltpu.get_barrier_semaphore()

    def greet(o):
        pl.semaphore_signal(
            barrier, inc=1, device_id=(z, lax.rem(me + o + 1, n)),
            device_id_type=pl.DeviceIdType.MESH,
        )

    def greet_z(o):
        pl.semaphore_signal(
            barrier, inc=1, device_id=(lax.rem(z + o + 1, g), me),
            device_id_type=pl.DeviceIdType.MESH,
        )

    loop(n - 1, greet)
    loop(g - 1, greet_z)

    def kv_head(h):
        kv_send[head(h), :] = dot_tn(k_ref[:, head(h)], v_ref[:, head(h)]).astype(BF16)

    loop(HEADS, kv_head)
    pl.semaphore_wait(barrier, n - 1 + g - 1)

    def spread(send, recv, ssem, rsem):
        def one(o):
            d = lax.rem(me + o + 1, n)
            to(send.at[part(d)], recv.at[me], ssem.at[d], rsem.at[me], d).start()

        loop(n - 1, one)
        recv[me] = send[part(me), :]

    def arrived(send, recv, ssem, rsem):
        def one(o):
            d = lax.rem(me + o + 1, n)
            to(send.at[part(d)], recv.at[d], ssem.at[d], rsem.at[d], d).wait()

        loop(n - 1, one)

    def sums(recv, pref, backward):
        def one(i, total):
            j = n - 1 - i if backward else i
            pref[j] = total.astype(BF16)
            return total + recv[j].astype(F32)

        lax.fori_loop(0, n, one, jnp.zeros((rows, HEAD_DIM), F32))

    def give_back(pref, dst, ssem, rsem):
        def one(o):
            d = lax.rem(me + o + 1, n)
            to(pref.at[d], dst.at[part(me)], ssem.at[d], rsem.at[me], d).start()

        loop(n - 1, one)
        dst[part(me), :] = pref[me]

    def given(pref, dst, ssem, rsem):
        def one(o):
            d = lax.rem(me + o + 1, n)
            to(pref.at[d], dst.at[part(d)], ssem.at[d], rsem.at[d], d).wait()

        loop(n - 1, one)

    spread(kv_send, kv_recv, s_kv1, r_kv1)

    def own_rows(c, device):
        return to(w_ref, wfull.at[part(me)], s_w.at[c], r_w.at[me], device)

    def send_rows(o):
        c = lax.rem(chip + o + 1, nc)
        own_rows(c, c * 2 + core).start()

    loop(nc - 1, send_rows)
    own_rows(chip, sibling).start()
    wfull[part(me), :] = w_ref[...]

    causal = lax.broadcasted_iota(jnp.int32, (tok, tok), 0) >= lax.broadcasted_iota(
        jnp.int32, (tok, tok), 1
    )

    def score_head(h):
        s = dot_nt(q_ref[:, head(h)], k_ref[:, head(h)]) * att_scale
        s = jnp.where(causal, s, 0.0).astype(BF16)
        scores[h] = s
        intra[:, head(h)] = dot_nn(s, v_ref[:, head(h)])

    loop(HEADS // 2, score_head)
    arrived(kv_send, kv_recv, s_kv1, r_kv1)
    sums(kv_recv, kv_pref, False)
    give_back(kv_pref, kvb, s_kv2, r_kv2)
    loop(HEADS // 2, lambda h: score_head(h + HEADS // 2))
    given(kv_pref, kvb, s_kv2, r_kv2)

    def attend_head(h):
        a = intra[:, head(h)] + att_scale * dot_nn(q_ref[:, head(h)], kvb[head(h), :])
        a = a.astype(BF16)
        att[:, head(h)] = a
        att_t[head(h), :] = a.T

    loop(HEADS, attend_head)

    def sib_copy(i):
        return to(sib_send.at[i], sib_recv.at[i], s_sib.at[i], r_sib.at[i], sibling)

    def chunk(i):
        q = lax.rem(z + 1 + i, g)
        wchunk[...] = dot_nn(att_t[...], og_ref[:, column(q)]) * grad_scale

        def split(c):
            keep[i, c] = wchunk[part(c * 2 + core), :]
            sib_send[i, c] = wchunk[part(c * 2 + 1 - core), :].astype(BF16)

        loop(nc, split)
        sib_copy(i).start()

    loop(g, chunk)

    def row_copy(c):
        return to(
            wfull.at[part(c * 2 + core)], wfull.at[part(c * 2 + core)],
            s_wf.at[c], r_w.at[c * 2 + core], sibling,
        )

    def hand_on(o):
        c = lax.rem(chip + o + 1, nc)
        d = c * 2 + core
        to(w_ref, wfull.at[part(d)], s_w.at[c], r_w.at[d], d).wait()
        row_copy(c).start()

    def x_copy(i, c, slot):
        return to(x_send.at[i, c], x_recv.at[i, slot], s_x.at[i, c], r_x.at[i, slot], c * 2 + core)

    def cross(i):
        sib_copy(i).wait()

        def one(o):
            c = lax.rem(chip + o + 1, nc)
            x_send[i, c] = (keep[i, c] + sib_recv[i, c].astype(F32)).astype(BF16)
            x_copy(i, c, chip).start()

        loop(nc - 1, one)
        keep[i, chip] = keep[i, chip] + sib_recv[i, chip].astype(F32)

    loop(g, cross)
    loop(nc - 1, hand_on)

    own_rows(chip, sibling).wait_send()
    to(w_ref, wfull.at[part(sibling)], s_w.at[chip], r_w.at[sibling], sibling).wait_recv()

    def handed(o):
        c = lax.rem(chip + o + 1, nc)
        d = c * 2 + 1 - core
        row_copy(c).wait_send()
        to(wfull.at[part(d)], wfull.at[part(d)], s_wf.at[c], r_w.at[d], sibling).wait_recv()

    loop(nc - 1, handed)

    def grad_pair(p):
        two = pl.ds(pl.multiple_of(p * 2 * HEAD_DIM, 2 * HEAD_DIM), 2 * HEAD_DIM)
        hg[:, two] = dot_nt(og_ref[...], wfull[two, :]).astype(BF16)

    loop(HEADS // 2, grad_pair)

    def qg_head(h):
        qg_send[head(h), :] = dot_tn(q_ref[:, head(h)], hg[:, head(h)]).astype(BF16)

    loop(HEADS, qg_head)
    spread(qg_send, qg_recv, s_qg1, r_qg1)

    def z_copy(i, group, slot):
        return to_z(z_send.at[i], z_recv.at[slot], s_z.at[i], r_z.at[slot], group)

    def collect(i):
        def one(o, total):
            c = lax.rem(chip + o + 1, nc)
            x_copy(i, c, c).wait()
            return total + x_recv[i, c].astype(F32)

        return lax.fori_loop(0, nc - 1, one, keep[i, chip])

    def to_owner(i):
        z_send[i] = collect(i).astype(BF16)
        z_copy(i, lax.rem(z + 1 + i, g), z).start()

    def back_head(h):
        hgh = hg[:, head(h)]
        b = dot_nt(hgh, v_ref[:, head(h)]) * att_scale
        b = jnp.where(causal, b, 0.0).astype(BF16)
        qgrad_ref[:, head(h)] = (
            dot_nn(b, k_ref[:, head(h)]) + att_scale * dot_nt(hgh, kvb[head(h), :])
        ).astype(BF16)
        intra[:, head(h)] = dot_tn(b, q_ref[:, head(h)])

    loop(HEADS, back_head)
    arrived(qg_send, qg_recv, s_qg1, r_qg1)
    sums(qg_recv, qg_pref, True)
    give_back(qg_pref, qga, s_qg2, r_qg2)

    loop(g - 1, to_owner)

    def output_pair(p):
        wide = pl.ds(pl.multiple_of(p * 512, 512), 512)
        out_ref[:, wide] = dot_nn(att[...], wfull[:, wide]).astype(BF16)

    loop(model // 512, output_pair)
    given(qg_pref, qga, s_qg2, r_qg2)

    def last_head(h):
        qgh = qga[head(h), :]
        kgrad_ref[:, head(h)] = (
            intra[:, head(h)] + att_scale * dot_nt(v_ref[:, head(h)], qgh)
        ).astype(BF16)
        vgrad_ref[:, head(h)] = (
            dot_tn(scores[h], hg[:, head(h)]) + att_scale * dot_nn(k_ref[:, head(h)], qgh)
        ).astype(BF16)

    loop(HEADS, last_head)

    def own_total(o, total):
        s = lax.rem(z + o + 1, g)
        z_copy(0, s, s).wait_recv()
        return total + z_recv[s].astype(F32)

    final = lax.fori_loop(0, g - 1, own_total, collect(g - 1)).astype(BF16)
    z2_send[...] = final

    def z2_copy(group, slot):
        return to_z(z2_send, z2_recv.at[slot], s_z2.at[group], r_z2.at[slot], group)

    loop(g - 1, lambda o: z2_copy(lax.rem(z + o + 1, g), z).start())
    wgrad_ref[:, column(z)] = final.astype(F32)

    def finish(o):
        s = lax.rem(z + o + 1, g)
        z_copy(o, s, z).wait_send()
        z2_copy(s, s).wait()
        wgrad_ref[:, column(s)] = z2_recv[s].astype(F32)

    loop(g - 1, finish)


def on_device(query_in, key_in, value_in, out_grad, out_weight):
    n, g = lax.axis_size("context"), lax.axis_size("dp")
    tok, width = query_in.shape[1:]
    model = out_grad.shape[2]
    rows, cols, nc = width // n, model // g, n // 2
    vmem, dma = pltpu.VMEM, pltpu.SemaphoreType.DMA
    state = [
        vmem((width, HEAD_DIM), BF16), vmem((n, rows, HEAD_DIM), BF16),
        vmem((n, rows, HEAD_DIM), BF16), vmem((width, HEAD_DIM), BF16),
    ]
    scratch = [
        vmem((width, model), BF16), *state, *state,
        vmem((HEADS, tok, tok), BF16), vmem((tok, width), F32), vmem((tok, width), BF16),
        vmem((width, tok), BF16), vmem((tok, width), BF16), vmem((width, cols), F32),
        vmem((g, nc, rows, cols), F32),
        *[vmem((g, nc, rows, cols), BF16)] * 4,
        vmem((g, rows, cols), BF16), vmem((g, rows, cols), BF16),
        vmem((rows, cols), BF16), vmem((g, rows, cols), BF16),
        *[dma((n,))] * 8,
        dma((nc,)), dma((nc,)), dma((n,)), dma((g,)), dma((g,)), dma((g, nc)), dma((g, nc)),
        dma((g,)), dma((g,)), dma((g,)), dma((g,)),
    ]
    whole = pl.BlockSpec(memory_space=pltpu.VMEM)
    grads = jax.ShapeDtypeStruct((tok, width), BF16)
    outs = pl.pallas_call(
        functools.partial(kernel, n, g),
        out_shape=(
            jax.ShapeDtypeStruct((tok, model), BF16), grads, grads, grads,
            jax.ShapeDtypeStruct((rows, model), F32),
        ),
        in_specs=[whole] * 5,
        out_specs=(whole,) * 5,
        scratch_shapes=scratch,
        compiler_params=pltpu.CompilerParams(
            collective_id=0, has_side_effects=True, vmem_limit_bytes=58 * 2**20
        ),
        name="layer",
    )(query_in[0], key_in[0], value_in[0], out_grad[0], out_weight)
    return tuple(o[None] for o in outs[:4]) + (outs[4],)


def solution(mesh):
    split = P("dp", "context", None)
    rows = P("context", None)
    return jax.shard_map(
        on_device,
        mesh=mesh,
        in_specs=(split,) * 4 + (rows,),
        out_specs=(split,) * 4 + (rows,),
        check_vma=False,
    )
```

time: 281 us -> 106 us (0.38)
  waiting for transfers between devices: 170 us -> 0 us
  Pallas kernels: 0 us -> 97.5 us
  matrix products: 50.2 us -> 0 us
  other arithmetic: 19.4 us -> 0 us
  local copies, waits for them, and re-layouts: 25.7 us -> 7.2 us
  between operations: 13.9 us -> 0.66 us
    all_gather x3 -> x0, waiting for transfers between devices: 107 us -> none  [the longest x2 68.5 us: prefix(): pieces = lax.all_gather(value, axis)]
    pallas_call x0 -> x1, Pallas kernels: none -> 97.5 us  [on_device(): pl.pallas_call(functools.partial(kernel, n, g), out_shape=(jax.ShapeDtype...]
    reduce_scatter x1 -> x0, waiting for transfers between devices: 50.7 us -> none  [on_device(): lax.psum_scatter((lax.dot_general(attended, grad_flat, (((0,), (0,)), (()...]
    dot_general x15 -> x0, matrix products: 50.2 us -> none  [the longest x1 5.52 us: on_device(): lax.dot_general(grad_flat, full_weight, (((1,), (1,)), ((), ())), preferr...]
    select_n x14 -> x0, other arithmetic: 17.2 us -> none  [turn(): return jnp.where(position < mine, longer, so_far)]
    psum x1 -> x0, waiting for transfers between devices: 11.6 us -> none  [on_device(): weight_grad = lax.psum(group_part, 'dp').astype(jnp.float32)]
    unnamed x22 -> x13, local copies, waits for them, and re-layouts: 15.4 us -> 7.2 us
    rev x1 -> x0, local copies, waits for them, and re-layouts: 4.67 us -> none  [prefix(): pieces = pieces[::-1]]
  transfers between devices with their start and end apart: 5 -> 0, of which waited for: 5 -> 0; matrix products, arithmetic and copies ran while one was open for 14% -> 0% of each run, Pallas kernels for 0% -> 0%
where the time goes in v1:
time: 106 us; the launch traced here: 105 us
  Pallas kernels  97.5 us (92%)
  local copies, waits for them, and re-layouts  7.2 us (7%)
    pallas_call x1, Pallas kernels, on_device(): pl.pallas_call(functools.partial(kernel, n, g), out_shape=(jax.ShapeDtype...  97.5 us
    unnamed x13, local copies, waits for them, and re-layouts  7.2 us

profile of v1, /device:TPU:0, one launch (start us, length us, event | category | flops | bytes accessed | tf_op | source)
XLA Modules:
  0.0 105.4 jit_solution(5959612050487417583)
XLA Ops:
  0.6 97.5 %layer.1 = (bf16[512,2048]{1,0:T(8,128)(2,1)}, bf16[512,1024]{1,0:T(8,128)(2,1)}, bf16[512,1024]{1,0:T(8,128)(2,1)}, bf16[512,1024]{1,0:T(8,128)(2,1)}, f32[128,2048]{1,0:T(8,128)}) custom-call(bf16[512,1024]{1,0:T(8,128)(2,1)} %bitcast.13, bf16[512,1024]{1,0:T(8,128)(2,1)} %bitcast.14, bf16[512,1024]{1,0:T(8,128)(2,1)} %bitcast.15, ...), custom_call_target="tpu_custom_call" | custom-call | tf_op jit(solution)/shard_map/layer/pallas_call | solution.py:336
  98.2 0.0 copy-start.3
  98.2 0.0 copy-start.2
  98.2 3.3 %copy.15 = bf16[1,512,2048]{2,1,0:T(8,128)(2,1)} copy(bf16[1,512,2048]{2,1,0:T(8,128)(2,1)} %bitcast.8) | data formatting | bytes 4194304
  101.5 0.0 copy-done.3
  101.5 0.0 copy-start.1
  101.5 1.0 copy.16
  102.5 0.0 copy-done.2
  102.5 0.0 copy-start
  102.5 1.0 copy.17
  103.4 0.0 copy-done.1
  103.4 1.0 copy.18
  104.4 0.0 copy-done
  104.4 1.0 copy.19
Async XLA Ops:
  98.2 3.3 %copy-start.3 = (bf16[512,1024]{1,0:T(8,128)(2,1)S(1)}, bf16[512,1024]{1,0:T(8,128)(2,1)}, u32[]{:S(2)}) copy-start(bf16[512,1024]{1,0:T(8,128)(2,1)} %get-tuple-element.11) | copy-start | bytes 3145732
  98.2 4.3 %copy-start.2 = (bf16[512,1024]{1,0:T(8,128)(2,1)S(1)}, bf16[512,1024]{1,0:T(8,128)(2,1)}, u32[]{:S(2)}) copy-start(bf16[512,1024]{1,0:T(8,128)(2,1)} %get-tuple-element.12) | copy-start | bytes 3145732
  101.5 1.9 %copy-start.1 = (bf16[512,1024]{1,0:T(8,128)(2,1)S(1)}, bf16[512,1024]{1,0:T(8,128)(2,1)}, u32[]{:S(2)}) copy-start(bf16[512,1024]{1,0:T(8,128)(2,1)} %get-tuple-element.13) | copy-start | bytes 3145732
  102.5 1.9 %copy-start = (f32[128,2048]{1,0:T(8,128)S(1)}, f32[128,2048]{1,0:T(8,128)}, u32[]{:S(2)}) copy-start(f32[128,2048]{1,0:T(8,128)} %get-tuple-element.24) | copy-start | bytes 3145732

commit v2 on v1

--- a/solution.py
+++ b/solution.py
@@ -183,7 +183,6 @@
         loop(nc, split)
         sib_copy(i).start()
 
-    loop(g, chunk)
 
     def row_copy(c):
         return to(
@@ -211,7 +210,14 @@
         loop(nc - 1, one)
         keep[i, chip] = keep[i, chip] + sib_recv[i, chip].astype(F32)
 
-    loop(g, cross)
+    chunk(0)
+
+    def overlap(i):
+        chunk(i + 1)
+        cross(i)
+
+    loop(g - 1, overlap)
+    cross(g - 1)
     loop(nc - 1, hand_on)
 
     own_rows(chip, sibling).wait_send()
@@ -261,18 +267,37 @@
         ).astype(BF16)
         intra[:, head(h)] = dot_tn(b, q_ref[:, head(h)])
 
-    loop(HEADS, back_head)
+    def back_some(i):
+        to_owner(i)
+        loop(heads_each, lambda h: back_head(i * heads_each + h))
+
+    heads_each = HEADS // g
+    loop(g - 1, back_some)
+    loop(heads_each, lambda h: back_head((g - 1) * heads_each + h))
+
+    def output_pair(p):
+        wide = pl.ds(pl.multiple_of(p * 512, 512), 512)
+        out_ref[:, wide] = dot_nn(att[...], wfull[:, wide]).astype(BF16)
+
+    loop(model // 512, output_pair)
     arrived(qg_send, qg_recv, s_qg1, r_qg1)
     sums(qg_recv, qg_pref, True)
     give_back(qg_pref, qga, s_qg2, r_qg2)
 
-    loop(g - 1, to_owner)
-
-    def output_pair(p):
-        wide = pl.ds(pl.multiple_of(p * 512, 512), 512)
-        out_ref[:, wide] = dot_nn(att[...], wfull[:, wide]).astype(BF16)
-
-    loop(model // 512, output_pair)
+    def own_total(o, total):
+        s = lax.rem(z + o + 1, g)
+        z_copy(0, s, s).wait_recv()
+        return total + z_recv[s].astype(F32)
+
+    final = lax.fori_loop(0, g - 1, own_total, collect(g - 1)).astype(BF16)
+    z2_send[...] = final
+
+    def z2_copy(group, slot):
+        return to_z(z2_send, z2_recv.at[slot], s_z2.at[group], r_z2.at[slot], group)
+
+    loop(g - 1, lambda o: z2_copy(lax.rem(z + o + 1, g), z).start())
+    wgrad_ref[:, column(z)] = final.astype(F32)
+
     given(qg_pref, qga, s_qg2, r_qg2)
 
     def last_head(h):
@@ -285,20 +310,6 @@
         ).astype(BF16)
 
     loop(HEADS, last_head)
-
-    def own_total(o, total):
-        s = lax.rem(z + o + 1, g)
-        z_copy(0, s, s).wait_recv()
-        return total + z_recv[s].astype(F32)
-
-    final = lax.fori_loop(0, g - 1, own_total, collect(g - 1)).astype(BF16)
-    z2_send[...] = final
-
-    def z2_copy(group, slot):
-        return to_z(z2_send, z2_recv.at[slot], s_z2.at[group], r_z2.at[slot], group)
-
-    loop(g - 1, lambda o: z2_copy(lax.rem(z + o + 1, g), z).start())
-    wgrad_ref[:, column(z)] = final.astype(F32)
 
     def finish(o):
         s = lax.rem(z + o + 1, g)

time: 106 us -> 93.4 us (0.88)
  Pallas kernels: 97.5 us -> 85.3 us
    pallas_call x1, Pallas kernels: 97.5 us -> 85.3 us  [on_device(): pl.pallas_call(functools.partial(kernel, n, g), out_shape=(jax.ShapeDtype...]
where the time goes in v2:
time: 93.4 us; the launch traced here: 93.2 us
  Pallas kernels  85.3 us (91%)
  local copies, waits for them, and re-layouts  7.2 us (8%)
    pallas_call x1, Pallas kernels, on_device(): pl.pallas_call(functools.partial(kernel, n, g), out_shape=(jax.ShapeDtype...  85.3 us
    unnamed x13, local copies, waits for them, and re-layouts  7.2 us

profile of v2, /device:TPU:0, one launch (start us, length us, event | category | flops | bytes accessed | tf_op | source)
XLA Modules:
  0.0 93.2 jit_solution(12294627000451884654)
XLA Ops:
  0.6 85.3 %layer.1 = (bf16[512,2048]{1,0:T(8,128)(2,1)}, bf16[512,1024]{1,0:T(8,128)(2,1)}, bf16[512,1024]{1,0:T(8,128)(2,1)}, bf16[512,1024]{1,0:T(8,128)(2,1)}, f32[128,2048]{1,0:T(8,128)}) custom-call(bf16[512,1024]{1,0:T(8,128)(2,1)} %bitcast.13, bf16[512,1024]{1,0:T(8,128)(2,1)} %bitcast.14, bf16[512,1024]{1,0:T(8,128)(2,1)} %bitcast.15, ...), custom_call_target="tpu_custom_call" | custom-call | tf_op jit(solution)/shard_map/layer/pallas_call | solution.py:347
  86.0 0.0 copy-start.3
  86.0 0.0 copy-start.2
  86.0 3.3 %copy.15 = bf16[1,512,2048]{2,1,0:T(8,128)(2,1)} copy(bf16[1,512,2048]{2,1,0:T(8,128)(2,1)} %bitcast.8) | data formatting | bytes 4194304
  89.3 0.0 copy-done.3
  89.3 0.0 copy-start.1
  89.3 1.0 %copy.16 = bf16[1,512,1024]{2,1,0:T(8,128)(2,1)} copy(bf16[1,512,1024]{2,1,0:T(8,128)(2,1)S(1)} %bitcast.12) | data formatting | bytes 2097152
  90.3 0.0 copy-done.2
  90.3 0.0 copy-start
  90.3 1.0 %copy.17 = bf16[1,512,1024]{2,1,0:T(8,128)(2,1)} copy(bf16[1,512,1024]{2,1,0:T(8,128)(2,1)S(1)} %bitcast.11) | data formatting | bytes 2097152
  91.2 0.0 copy-done.1
  91.2 1.0 %copy.18 = bf16[1,512,1024]{2,1,0:T(8,128)(2,1)} copy(bf16[1,512,1024]{2,1,0:T(8,128)(2,1)S(1)} %bitcast.10) | data formatting | bytes 2097152
  92.2 0.0 copy-done
  92.2 1.0 %copy.19 = f32[128,2048]{1,0:T(8,128)} copy(f32[128,2048]{1,0:T(8,128)S(1)} %copy-done) | data formatting | bytes 2097152
Async XLA Ops:
  86.0 3.3 %copy-start.3 = (bf16[512,1024]{1,0:T(8,128)(2,1)S(1)}, bf16[512,1024]{1,0:T(8,128)(2,1)}, u32[]{:S(2)}) copy-start(bf16[512,1024]{1,0:T(8,128)(2,1)} %get-tuple-element.11) | copy-start | bytes 3145732
  86.0 4.3 %copy-start.2 = (bf16[512,1024]{1,0:T(8,128)(2,1)S(1)}, bf16[512,1024]{1,0:T(8,128)(2,1)}, u32[]{:S(2)}) copy-start(bf16[512,1024]{1,0:T(8,128)(2,1)} %get-tuple-element.12) | copy-start | bytes 3145732
  89.3 1.9 %copy-start.1 = (bf16[512,1024]{1,0:T(8,128)(2,1)S(1)}, bf16[512,1024]{1,0:T(8,128)(2,1)}, u32[]{:S(2)}) copy-start(bf16[512,1024]{1,0:T(8,128)(2,1)} %get-tuple-element.13) | copy-start | bytes 3145732
  90.3 1.9 %copy-start = (f32[128,2048]{1,0:T(8,128)S(1)}, f32[128,2048]{1,0:T(8,128)}, u32[]{:S(2)}) copy-start(f32[128,2048]{1,0:T(8,128)} %get-tuple-element.24) | copy-start | bytes 3145732

commit v3 on v2

--- a/solution.py
+++ b/solution.py
@@ -36,7 +36,7 @@
     scores, intra, att, att_t, hg, wchunk, keep, sib_send, sib_recv, x_send, x_recv,
     z_send, z_recv, z2_send, z2_recv,
     s_kv1, r_kv1, s_kv2, r_kv2, s_qg1, r_qg1, s_qg2, r_qg2,
-    s_w, s_wf, r_w, s_sib, r_sib, s_x, r_x, s_z, r_z, s_z2, r_z2,
+    s_w, s_wf, r_w, s_d, r_d, s_sib, r_sib, s_x, r_x, s_z, r_z, s_z2, r_z2,
 ):
     me, z = lax.axis_index("context"), lax.axis_index("dp")
     nc = n // 2
@@ -133,14 +133,27 @@
 
     spread(kv_send, kv_recv, s_kv1, r_kv1)
 
+    across = max(d for d in range(1, math.isqrt(nc) + 1) if nc % d == 0)
+    down = nc // across
+    cy, cx = chip // across, lax.rem(chip, across)
+
+    def beside(o):
+        return cy * across + lax.rem(cx + o + 1, across)
+
+    def below(o):
+        return lax.rem(cy + o + 1, down) * across + cx
+
+    def corner(o, p):
+        return lax.rem(cy + p + 1, down) * across + lax.rem(cx + o + 1, across)
+
     def own_rows(c, device):
         return to(w_ref, wfull.at[part(me)], s_w.at[c], r_w.at[me], device)
 
-    def send_rows(o):
-        c = lax.rem(chip + o + 1, nc)
+    def send_rows(c):
         own_rows(c, c * 2 + core).start()
 
-    loop(nc - 1, send_rows)
+    loop(across - 1, lambda o: send_rows(beside(o)))
+    loop(down - 1, lambda p: send_rows(below(p)))
     own_rows(chip, sibling).start()
     wfull[part(me), :] = w_ref[...]
 
@@ -190,10 +203,33 @@
             s_wf.at[c], r_w.at[c * 2 + core], sibling,
         )
 
-    def hand_on(o):
-        c = lax.rem(chip + o + 1, nc)
+    def hand_on(c):
         d = c * 2 + core
         to(w_ref, wfull.at[part(d)], s_w.at[c], r_w.at[d], d).wait()
+        row_copy(c).start()
+
+    def half_copy(half, shard, slot, device):
+        piece = wfull.at[part(shard * 2 + core), pl.ds(half * (model // 2), model // 2)]
+        return to(piece, piece, s_d.at[half, slot], r_d.at[half, shard], device * 2 + core)
+
+    def pass_beside(o):
+        hand_on(beside(o))
+        loop(
+            down - 1,
+            lambda p: half_copy(0, beside(o), corner(o, p), below(p)).start(),
+        )
+
+    def pass_below(p):
+        hand_on(below(p))
+        loop(
+            across - 1,
+            lambda o: half_copy(1, below(p), corner(o, p), beside(o)).start(),
+        )
+
+    def pass_corner(o, p):
+        c = corner(o, p)
+        half_copy(0, c, c, below(p)).wait()
+        half_copy(1, c, c, beside(o)).wait()
         row_copy(c).start()
 
     def x_copy(i, c, slot):
@@ -211,6 +247,8 @@
         keep[i, chip] = keep[i, chip] + sib_recv[i, chip].astype(F32)
 
     chunk(0)
+    loop(across - 1, pass_beside)
+    loop(down - 1, pass_below)
 
     def overlap(i):
         chunk(i + 1)
@@ -218,7 +256,7 @@
 
     loop(g - 1, overlap)
     cross(g - 1)
-    loop(nc - 1, hand_on)
+    loop(across - 1, lambda o: loop(down - 1, lambda p: pass_corner(o, p)))
 
     own_rows(chip, sibling).wait_send()
     to(w_ref, wfull.at[part(sibling)], s_w.at[chip], r_w.at[sibling], sibling).wait_recv()
@@ -339,7 +377,7 @@
         vmem((g, rows, cols), BF16), vmem((g, rows, cols), BF16),
         vmem((rows, cols), BF16), vmem((g, rows, cols), BF16),
         *[dma((n,))] * 8,
-        dma((nc,)), dma((nc,)), dma((n,)), dma((g,)), dma((g,)), dma((g, nc)), dma((g, nc)),
+        dma((nc,)), dma((nc,)), dma((n,)), dma((2, nc)), dma((2, nc)), dma((g,)), dma((g,)), dma((g, nc)), dma((g, nc)),
         dma((g,)), dma((g,)), dma((g,)), dma((g,)),
     ]
     whole = pl.BlockSpec(memory_space=pltpu.VMEM)

time: 93.4 us -> 86.2 us (0.923)
  Pallas kernels: 85.3 us -> 78.2 us
    pallas_call x1, Pallas kernels: 85.3 us -> 78.2 us  [on_device(): pl.pallas_call(functools.partial(kernel, n, g), out_shape=(jax.ShapeDtype...]
where the time goes in v3:
time: 86.2 us; the launch traced here: 86.1 us
  Pallas kernels  78.2 us (91%)
  local copies, waits for them, and re-layouts  7.2 us (8%)
    pallas_call x1, Pallas kernels, on_device(): pl.pallas_call(functools.partial(kernel, n, g), out_shape=(jax.ShapeDtype...  78.2 us
    unnamed x13, local copies, waits for them, and re-layouts  7.2 us

profile of v3, /device:TPU:0, one launch (start us, length us, event | category | flops | bytes accessed | tf_op | source)
XLA Modules:
  0.0 86.1 jit_solution(11365173722226383895)
XLA Ops:
  0.6 78.2 %layer.1 = (bf16[512,2048]{1,0:T(8,128)(2,1)}, bf16[512,1024]{1,0:T(8,128)(2,1)}, bf16[512,1024]{1,0:T(8,128)(2,1)}, bf16[512,1024]{1,0:T(8,128)(2,1)}, f32[128,2048]{1,0:T(8,128)}) custom-call(bf16[512,1024]{1,0:T(8,128)(2,1)} %bitcast.13, bf16[512,1024]{1,0:T(8,128)(2,1)} %bitcast.14, bf16[512,1024]{1,0:T(8,128)(2,1)} %bitcast.15, ...), custom_call_target="tpu_custom_call" | custom-call | tf_op jit(solution)/shard_map/layer/pallas_call | solution.py:385
  78.8 0.0 copy-start.3
  78.8 0.0 copy-start.2
  78.9 3.3 %copy.15 = bf16[1,512,2048]{2,1,0:T(8,128)(2,1)} copy(bf16[1,512,2048]{2,1,0:T(8,128)(2,1)} %bitcast.8) | data formatting | bytes 4194304
  82.2 0.0 copy-done.3
  82.2 0.0 copy-start.1
  82.2 1.0 %copy.16 = bf16[1,512,1024]{2,1,0:T(8,128)(2,1)} copy(bf16[1,512,1024]{2,1,0:T(8,128)(2,1)S(1)} %bitcast.12) | data formatting | bytes 2097152
  83.1 0.0 copy-done.2
  83.1 0.0 copy-start
  83.1 1.0 %copy.17 = bf16[1,512,1024]{2,1,0:T(8,128)(2,1)} copy(bf16[1,512,1024]{2,1,0:T(8,128)(2,1)S(1)} %bitcast.11) | data formatting | bytes 2097152
  84.1 0.0 copy-done.1
  84.1 1.0 %copy.18 = bf16[1,512,1024]{2,1,0:T(8,128)(2,1)} copy(bf16[1,512,1024]{2,1,0:T(8,128)(2,1)S(1)} %bitcast.10) | data formatting | bytes 2097152
  85.1 0.0 copy-done
  85.1 1.0 %copy.19 = f32[128,2048]{1,0:T(8,128)} copy(f32[128,2048]{1,0:T(8,128)S(1)} %copy-done) | data formatting | bytes 2097152
Async XLA Ops:
  78.8 3.3 %copy-start.3 = (bf16[512,1024]{1,0:T(8,128)(2,1)S(1)}, bf16[512,1024]{1,0:T(8,128)(2,1)}, u32[]{:S(2)}) copy-start(bf16[512,1024]{1,0:T(8,128)(2,1)} %get-tuple-element.11) | copy-start | bytes 3145732
  78.8 4.3 %copy-start.2 = (bf16[512,1024]{1,0:T(8,128)(2,1)S(1)}, bf16[512,1024]{1,0:T(8,128)(2,1)}, u32[]{:S(2)}) copy-start(bf16[512,1024]{1,0:T(8,128)(2,1)} %get-tuple-element.12) | copy-start | bytes 3145732
  82.2 1.9 %copy-start.1 = (bf16[512,1024]{1,0:T(8,128)(2,1)S(1)}, bf16[512,1024]{1,0:T(8,128)(2,1)}, u32[]{:S(2)}) copy-start(bf16[512,1024]{1,0:T(8,128)(2,1)} %get-tuple-element.13) | copy-start | bytes 3145732
  83.1 1.9 %copy-start = (f32[128,2048]{1,0:T(8,128)S(1)}, f32[128,2048]{1,0:T(8,128)}, u32[]{:S(2)}) copy-start(f32[128,2048]{1,0:T(8,128)} %get-tuple-element.24) | copy-start | bytes 3145732

commit v4 on v3

--- a/solution.py
+++ b/solution.py
@@ -313,11 +313,6 @@
     loop(g - 1, back_some)
     loop(heads_each, lambda h: back_head((g - 1) * heads_each + h))
 
-    def output_pair(p):
-        wide = pl.ds(pl.multiple_of(p * 512, 512), 512)
-        out_ref[:, wide] = dot_nn(att[...], wfull[:, wide]).astype(BF16)
-
-    loop(model // 512, output_pair)
     arrived(qg_send, qg_recv, s_qg1, r_qg1)
     sums(qg_recv, qg_pref, True)
     give_back(qg_pref, qga, s_qg2, r_qg2)
@@ -336,6 +331,11 @@
     loop(g - 1, lambda o: z2_copy(lax.rem(z + o + 1, g), z).start())
     wgrad_ref[:, column(z)] = final.astype(F32)
 
+    def output_pair(p):
+        wide = pl.ds(pl.multiple_of(p * 512, 512), 512)
+        out_ref[:, wide] = dot_nn(att[...], wfull[:, wide]).astype(BF16)
+
+    loop(model // 512, output_pair)
     given(qg_pref, qga, s_qg2, r_qg2)
 
     def last_head(h):

time: 86.2 us -> 86.2 us (level)
  no operation moved by 1% of the time
where the time goes in v4:
time: 86.2 us; the launch traced here: 86.1 us
  Pallas kernels  78.2 us (91%)
  local copies, waits for them, and re-layouts  7.2 us (8%)
    pallas_call x1, Pallas kernels, on_device(): pl.pallas_call(functools.partial(kernel, n, g), out_shape=(jax.ShapeDtype...  78.2 us
    unnamed x13, local copies, waits for them, and re-layouts  7.2 us

profile of v4, /device:TPU:0, one launch (start us, length us, event | category | flops | bytes accessed | tf_op | source)
XLA Modules:
  0.0 86.1 jit_solution(7557763655675094583)
XLA Ops:
  0.6 78.2 %layer.1 = (bf16[512,2048]{1,0:T(8,128)(2,1)}, bf16[512,1024]{1,0:T(8,128)(2,1)}, bf16[512,1024]{1,0:T(8,128)(2,1)}, bf16[512,1024]{1,0:T(8,128)(2,1)}, f32[128,2048]{1,0:T(8,128)}) custom-call(bf16[512,1024]{1,0:T(8,128)(2,1)} %bitcast.13, bf16[512,1024]{1,0:T(8,128)(2,1)} %bitcast.14, bf16[512,1024]{1,0:T(8,128)(2,1)} %bitcast.15, ...), custom_call_target="tpu_custom_call" | custom-call | tf_op jit(solution)/shard_map/layer/pallas_call | solution.py:385
  78.8 0.0 copy-start.3
  78.8 0.0 copy-start.2
  78.9 3.3 %copy.15 = bf16[1,512,2048]{2,1,0:T(8,128)(2,1)} copy(bf16[1,512,2048]{2,1,0:T(8,128)(2,1)} %bitcast.8) | data formatting | bytes 4194304
  82.2 0.0 copy-done.3
  82.2 0.0 copy-start.1
  82.2 1.0 %copy.16 = bf16[1,512,1024]{2,1,0:T(8,128)(2,1)} copy(bf16[1,512,1024]{2,1,0:T(8,128)(2,1)S(1)} %bitcast.12) | data formatting | bytes 2097152
  83.1 0.0 copy-done.2
  83.1 0.0 copy-start
  83.1 1.0 %copy.17 = bf16[1,512,1024]{2,1,0:T(8,128)(2,1)} copy(bf16[1,512,1024]{2,1,0:T(8,128)(2,1)S(1)} %bitcast.11) | data formatting | bytes 2097152
  84.1 0.0 copy-done.1
  84.1 1.0 %copy.18 = bf16[1,512,1024]{2,1,0:T(8,128)(2,1)} copy(bf16[1,512,1024]{2,1,0:T(8,128)(2,1)S(1)} %bitcast.10) | data formatting | bytes 2097152
  85.1 0.0 copy-done
  85.1 1.0 %copy.19 = f32[128,2048]{1,0:T(8,128)} copy(f32[128,2048]{1,0:T(8,128)S(1)} %copy-done) | data formatting | bytes 2097152
Async XLA Ops:
  78.8 3.3 %copy-start.3 = (bf16[512,1024]{1,0:T(8,128)(2,1)S(1)}, bf16[512,1024]{1,0:T(8,128)(2,1)}, u32[]{:S(2)}) copy-start(bf16[512,1024]{1,0:T(8,128)(2,1)} %get-tuple-element.11) | copy-start | bytes 3145732
  78.8 4.3 %copy-start.2 = (bf16[512,1024]{1,0:T(8,128)(2,1)S(1)}, bf16[512,1024]{1,0:T(8,128)(2,1)}, u32[]{:S(2)}) copy-start(bf16[512,1024]{1,0:T(8,128)(2,1)} %get-tuple-element.12) | copy-start | bytes 3145732
  82.2 1.9 %copy-start.1 = (bf16[512,1024]{1,0:T(8,128)(2,1)S(1)}, bf16[512,1024]{1,0:T(8,128)(2,1)}, u32[]{:S(2)}) copy-start(bf16[512,1024]{1,0:T(8,128)(2,1)} %get-tuple-element.13) | copy-start | bytes 3145732
  83.1 1.9 %copy-start = (f32[128,2048]{1,0:T(8,128)S(1)}, f32[128,2048]{1,0:T(8,128)}, u32[]{:S(2)}) copy-start(f32[128,2048]{1,0:T(8,128)} %get-tuple-element.24) | copy-start | bytes 3145732
